TPU v7x, 32 devices: a whole 2x2x4 slice. The times are simulated.
32 devices in a mesh: gx: 8 (over z, x), gy: 4 (over y, core).
Axes of the slice: x: 2, y: 2, z: 4, core: 2. Of those that a mesh axis runs over, the one named last changes fastest.
Arguments:
- rhs: float32 [48, 32, 192], P('gx', 'gy'), may hold values from -6 to 6
- diag_blocks: float32 [48, 32, 192, 192], P('gx', 'gy'), as said below
- east_blocks: float32 [48, 32, 192, 192], P('gx', 'gy')
- north_blocks: float32 [48, 32, 192, 192], P('gx', 'gy')
- face_open: int32 [48, 32, 2], P('gx', 'gy'), may hold values 0 or 1
- modes: float32 [48, 32, 6, 192], P('gx', 'gy'), may hold values from -0.21875 to 0.21875
- aggregate: int32 [48, 32], P('gx', 'gy'), may hold values from 0 to 15, as said below
- live_count: int32 [8, 4], P('gx', 'gy'), may hold values from 8 to 16, as said below
Outputs:
- smoothed: float32 [48, 32, 192], P('gx', 'gy')
- coarse_rows: float32 [8, 4, 64, 6, 288], P('gx', 'gy')
- coarse_rhs: float32 [8, 4, 64, 6], P('gx', 'gy')
Inputs may be any that keep to these rules, and one draw needn't show every extreme that they name: `live_count`: some device has exactly 16 aggregates in use in every draw. `aggregate`: each element's slot is below its device's live_count. diag_blocks are symmetric.
All inputs are finite; a program needn't handle non-finite values. No bound on the sum of `face_open` on one device may be relied on, other than what follows from the above.
Results may differ from a plain program's by a relative error of at most 0.0003.
Values sent between devices are 32-bit elements; how exact they have to be, the bound alone decides.
A program may use at most 384 MiB of HBM per device.

v0:
```python
import functools

import jax
import jax.numpy as jnp
from jax import lax
from jax.experimental import pallas as pl
from jax.experimental.pallas import tpu as pltpu
from jax.sharding import PartitionSpec as P

MODES = 6
CHEB = 4
AGG_DEV = 16
PASSES = CHEB + 1
F32 = jnp.float32
BF16 = jnp.bfloat16
NN = (((1,), (0,)), ((), ()))
NT = (((1,), (1,)), ((), ()))


def split(value):
    high = value.astype(BF16)
    return high, (value - high.astype(F32)).astype(BF16)


def mul(a, b, dims):
    return lax.dot_general(a, b, dims, preferred_element_type=F32)


def mul_split(a, b, dims):
    a_high, a_low = split(a)
    b_high, b_low = split(b)
    return mul(a_high, b_high, dims) + (mul(a_low, b_high, dims) + mul(a_high, b_low, dims))


def mul_left_hot(hot, b):
    b_high, b_low = split(b)
    hot = hot.astype(BF16)
    return mul(hot, b_high, NN) + mul(hot, b_low, NN)


def mul_right_hot(a, hot):
    a_high, a_low = split(a)
    hot = hot.astype(BF16)
    return mul(a_high, hot, NN) + mul(a_low, hot, NN)


def iota(shape, dim):
    return lax.broadcasted_iota(jnp.int32, shape, dim)


def kernel(
    sizes,
    rhs, diag_hbm, east_hbm, north_hbm, face, modes, aggregate, live,
    x_out, rows_out, crhs_out,
    diag, east, north, inv, field, ahead, back_x, back_y, step_ref, coef,
    wall, hot6, hot8, hot_at, wide_hot, r_diag, r_east, r_north,
    w_stage, q_stage, v_stage, y_stage,
    v_east, v_north, b_west, b_south,
    sum_own, sum_own2, sum_gy, sum_gx, gath, gath2, rows_own, crhs_own, proj,
    load_sem, halo_send, halo_recv, mode_send, mode_recv,
    gy_send, gy_recv, gx_send, gx_recv, rows_send, rows_recv, crhs_send, crhs_recv,
):
    gxs, gys, ex, ey, nb = sizes
    ne = ex * ey
    slots = ne + 16
    cap = gys * AGG_DEV
    g = lax.axis_index("gx")
    q = lax.axis_index("gy")

    loads = {}
    for i in range(ex):
        for k, (src, dst) in enumerate(((diag_hbm, diag), (east_hbm, east), (north_hbm, north))):
            loads[i, k] = pltpu.make_async_copy(src.at[i], dst.at[i], load_sem.at[i, k])
            loads[i, k].start()

    v_east[...] = jnp.zeros_like(v_east)
    v_north[...] = jnp.zeros_like(v_north)
    b_west[...] = jnp.zeros_like(b_west)
    b_south[...] = jnp.zeros_like(b_south)
    wall[ne:] = jnp.zeros((16, 8, nb), F32)
    hot6[ne:] = jnp.zeros((16, 8, 128), F32)
    v_stage[...] = jnp.zeros_like(v_stage)
    y_stage[...] = jnp.zeros_like(y_stage)

    barrier = pltpu.get_barrier_semaphore()
    for k in range(1, gys):
        pl.semaphore_signal(barrier, inc=1, device_id={"gy": lax.rem(q + k, gys)}, device_id_type=pl.DeviceIdType.MESH)
    for k in range(1, gxs):
        pl.semaphore_signal(barrier, inc=1, device_id={"gx": lax.rem(g + k, gxs)}, device_id_type=pl.DeviceIdType.MESH)

    sub = iota((8, 128), 0)
    lane = iota((8, 128), 1)
    sub3 = iota((8, 384), 0)
    lane3 = iota((8, 384), 1)

    def prepare(i, _):
        for j in range(ey):
            e = i * ey + j
            slot = aggregate[i, j]
            wall[e] = jnp.concatenate([modes[i, j], jnp.zeros((8 - MODES, nb), F32)], 0)
            hot6[e] = jnp.where((lane == MODES * slot + sub) & (sub < MODES), 1.0, 0.0)
            hot8[e] = jnp.where(lane == 8 * slot + sub, 1.0, 0.0)
            hot_at[e] = jnp.where(lane == slot, 1.0, 0.0)
            wide_hot[e] = jnp.where((lane3 == MODES * slot + sub3) & (sub3 < MODES), 1.0, 0.0)
        w_stage[i] = wall[i * ey]
        q_stage[i] = hot6[i * ey]
        return 0

    lax.fori_loop(0, ex, prepare, 0)
    field[...] = jnp.zeros_like(field)
    field[0:ex, 0:ey] = rhs[...]

    pl.semaphore_wait(barrier, gxs + gys - 2)

    def remote(src, dst, send, recv, **where):
        return pltpu.make_async_remote_copy(
            src_ref=src, dst_ref=dst, send_sem=send, recv_sem=recv,
            device_id=where, device_id_type=pl.DeviceIdType.MESH,
        )

    has_west, has_east = g > 0, g < gxs - 1
    has_south, has_north = q > 0, q < gys - 1
    west, east_g = jnp.maximum(g - 1, 0), jnp.minimum(g + 1, gxs - 1)
    south, north_q = jnp.maximum(q - 1, 0), jnp.minimum(q + 1, gys - 1)

    mode_copies = (
        (has_west, has_east, remote(wall.at[pl.ds(0, ey)], wall.at[pl.ds(ne, ey)], mode_send.at[0], mode_recv.at[0], gx=west)),
        (has_west, has_east, remote(hot6.at[pl.ds(0, ey)], hot6.at[pl.ds(ne, ey)], mode_send.at[1], mode_recv.at[1], gx=west)),
        (has_south, has_north, remote(w_stage, wall.at[pl.ds(ne + 8, ex)], mode_send.at[2], mode_recv.at[2], gy=south)),
        (has_south, has_north, remote(q_stage, hot6.at[pl.ds(ne + 8, ex)], mode_send.at[3], mode_recv.at[3], gy=south)),
    )
    for sends, _, copy in mode_copies:
        pl.when(sends)(copy.start)

    same = iota((nb, nb), 0) == iota((nb, nb), 1)

    def coarse_row(i, _):
        for k, (src, dst) in enumerate(((diag_hbm, diag), (east_hbm, east), (north_hbm, north))):
            pltpu.make_async_copy(src.at[i], dst.at[i], load_sem.at[i, k]).wait()
        for j in range(ey):
            e = i * ey + j
            main = jnp.sum(jnp.where(same, diag[i, j], 0.0), axis=0, keepdims=True)
            inv[i, pl.ds(j, 1), :] = 1.0 / main
            w = wall[e]
            w_high = w.astype(BF16).astype(F32)
            both = jnp.concatenate([w_high, w - w_high], 0).astype(BF16)
            for block, result, scale in (
                (diag, r_diag, None),
                (east, r_east, face[i, j, 0].astype(F32)),
                (north, r_north, face[i, j, 1].astype(F32)),
            ):
                high, low = split(block[i, j])
                product = mul(both, high, NN) + mul(both, low, NN)
                product = product[:8] + product[8:]
                result[e] = product if scale is None else product * scale
        return 0

    lax.fori_loop(0, ex, coarse_row, 0)

    for sends, receives, copy in mode_copies:
        pl.when(receives)(copy.wait_recv)
        pl.when(sends)(copy.wait_send)

    shape = (ne * 8, slots * 8)
    row_e = lax.shift_right_logical(iota(shape, 0), 3)
    col_e = lax.shift_right_logical(iota(shape, 1), 3)
    row_j = row_e & (ey - 1)
    row_i = lax.shift_right_logical(row_e, ey.bit_length() - 1)
    w_all = wall[...].reshape(slots * 8, nb)
    on_main = mul_split(r_diag[...].reshape(ne * 8, nb), w_all, NT)
    on_east = mul_split(r_east[...].reshape(ne * 8, nb), w_all, NT)
    on_north = mul_split(r_north[...].reshape(ne * 8, nb), w_all, NT)
    next_y = jnp.where(row_j < ey - 1, row_e + 1, ne + 8 + row_i)
    coupling = jnp.where(col_e == row_e + ey, on_east, 0.0) + jnp.where(col_e == next_y, on_north, 0.0)
    main_part = jnp.where(col_e == row_e, on_main, 0.0) + coupling
    halo_x = jnp.concatenate([hot6[ne : ne + 8].reshape(64, 128), jnp.zeros((64, 256), F32)], 1)
    halo_y = jnp.concatenate([hot6[ne + 8 :].reshape(64, 128), jnp.zeros((64, 256), F32)], 1)
    wide_hot[ne : ne + 8] = pltpu.roll(halo_x, 96, 1).reshape(8, 8, 384)
    wide_hot[ne + 8 :] = pltpu.roll(halo_y, 192, 1).reshape(8, 8, 384)
    wide = wide_hot[...].reshape(slots * 8, 384)
    spread = mul_right_hot(main_part, wide)
    spread = spread + mul_right_hot(coupling[:, : ne * 8].T, wide[: ne * 8])
    hot8_t = hot8[...].reshape(ne * 8, 128).T
    rows = mul_left_hot(hot8_t, spread)
    count = live[0, 0].astype(F32)
    rows_own[...] = jnp.where(iota(rows.shape, 1) >= 288, count, rows)

    rows_copy = remote(rows_own, gath.at[q], rows_send, rows_recv.at[q], gy=0 * q)
    pl.when(q > 0)(rows_copy.start)

    sum_copies_gy = [
        remote(sum_own, sum_gy.at[k - 1], gy_send.at[k - 1], gy_recv.at[k - 1], gy=lax.rem(q + k, gys))
        for k in range(1, gys)
    ]
    sum_copies_gx = [
        remote(sum_own2, sum_gx.at[k - 1], gx_send.at[k - 1], gx_recv.at[k - 1], gx=lax.rem(g + k, gxs))
        for k in range(1, gxs)
    ]

    def backs(i, j):
        own = field[i, pl.ds(j, 1), :]
        column = jnp.broadcast_to(own, (128, nb)).T
        short = column[:, : nb - 128]
        ox = face[i, j, 0].astype(F32)
        oy = face[i, j, 1].astype(F32)
        for block, result, at, scale in (
            (east, back_x, (i + 1, pl.ds(j, 1)), ox),
            (north, back_y, (i, pl.ds(j + 1, 1)), oy),
        ):
            result[at + (slice(0, 128),)] = scale * jnp.sum(block[i, j, :, 0:128] * column, axis=0, keepdims=True)
            result[at + (slice(128, nb),)] = scale * jnp.sum(block[i, j, :, 128:nb] * short, axis=0, keepdims=True)

    def aheads(i, j):
        ox = face[i, j, 0].astype(F32)
        oy = face[i, j, 1].astype(F32)
        own = field[i, pl.ds(j, 1), :]
        ve = field[i + 1, pl.ds(j, 1), :] * ox
        vn = field[i, pl.ds(j + 1, 1), :] * oy

        def part(s, t):
            cut = slice(s, t)
            return (
                diag[i, j, :, cut] * own[:, cut]
                + east[i, j, :, cut] * ve[:, cut]
                + north[i, j, :, cut] * vn[:, cut]
            )

        rest = jnp.concatenate([part(128, nb), jnp.zeros((nb, 256 - nb), F32)], 1)
        total = part(0, 128) + rest
        ahead[i, pl.ds(j, 1), :] = jnp.sum(total.T, axis=0, keepdims=True)

    last_x, last_y = ex - 1, ey - 1

    def one_pass(k, _):
        for i in range(ex):
            v_stage[pl.ds(i, 1), :] = field[i, 0:1, :]
        go_w = remote(field.at[0, pl.ds(0, ey)], v_east.at[k], halo_send.at[k, 0], halo_recv.at[k, 0], gx=west)
        go_s = remote(v_stage, v_north.at[k], halo_send.at[k, 1], halo_recv.at[k, 1], gy=south)
        go_e = remote(back_x.at[ex], b_west.at[k], halo_send.at[k, 2], halo_recv.at[k, 2], gx=east_g)
        go_n = remote(y_stage, b_south.at[k], halo_send.at[k, 3], halo_recv.at[k, 3], gy=north_q)
        pl.when(has_west)(go_w.start)
        pl.when(has_south)(go_s.start)
        for j in range(ey):
            backs(last_x, j)
        pl.when(has_east)(go_e.start)
        for i in range(last_x):
            backs(i, last_y)
        for i in range(ex):
            y_stage[pl.ds(i, 1), :] = back_y[i, ey : ey + 1, :]
        pl.when(has_north)(go_n.start)

        def inner(i, _):
            for j in range(last_y):
                backs(i, j)
                aheads(i, j)
            return 0

        lax.fori_loop(0, last_x, inner, 0)

        @pl.when(k == 1)
        def _():
            total = sum_own[...]
            for n, copy in enumerate(sum_copies_gy):
                copy.wait()
                total = total + sum_gy[n]
            sum_own2[...] = total
            for copy in sum_copies_gx:
                copy.start()

        pl.when(has_east)(go_w.wait_recv)
        pl.when(has_north)(go_s.wait_recv)
        field[ex, 0:ey] = v_east[k]
        for i in range(ex):
            field[i, ey : ey + 1, :] = v_north[k, i : i + 1, :]
        for j in range(ey):
            aheads(last_x, j)
        for i in range(last_x):
            aheads(i, last_y)
        pl.when(has_west)(go_e.wait_recv)
        pl.when(has_south)(go_n.wait_recv)
        back_x[0] = b_west[k]
        for i in range(ex):
            back_y[i, 0:1, :] = b_south[k, i : i + 1, :]
        pl.when(has_west)(go_w.wait_send)
        pl.when(has_south)(go_s.wait_send)
        pl.when(has_east)(go_e.wait_send)
        pl.when(has_north)(go_n.wait_send)
        applied = ahead[...] + back_x[0:ex] + back_y[:, 0:ey]
        ahead[...] = applied

        @pl.when(k == 0)
        def _():
            scaled = inv[...] * applied
            base = rhs[...]

            def fold(value):
                value = jnp.sum(value * value, axis=0)
                rest = jnp.concatenate([value[:, 128:], jnp.zeros((ey, 256 - nb), F32)], 1)
                return value[:, :128] + rest

            sum_own[0] = fold(scaled)
            sum_own[1] = fold(base)
            for copy in sum_copies_gy:
                copy.start()
            field[0:ex, 0:ey] = inv[...] * base

        @pl.when(k == 1)
        def _():
            total = sum_own2[...]
            for n, copy in enumerate(sum_copies_gx):
                copy.wait()
                total = total + sum_gx[n]
            top = jnp.sum(jnp.sum(total[0], axis=1, keepdims=True), axis=0, keepdims=True)
            bottom = jnp.sum(jnp.sum(total[1], axis=1, keepdims=True), axis=0, keepdims=True)
            lam = jnp.broadcast_to(jnp.sqrt(top / (bottom + 1e-06)), (1, nb))
            upper = 1.1 * lam
            lower = 0.3 * lam
            theta = 0.5 * (upper + lower)
            delta = 0.5 * (upper - lower)
            sigma = theta / delta
            coef[0:1] = sigma
            coef[1:2] = delta
            coef[2:3] = 1.0 / sigma
            start = field[0:ex, 0:ey] / theta.reshape(1, 1, nb)
            step_ref[...] = start
            field[0:ex, 0:ey] = start
            ahead[...] = ahead[...] / theta.reshape(1, 1, nb)

        @pl.when((k >= 1) & (k < PASSES - 1))
        def _():
            resid = rhs[...] - ahead[...]
            sigma, delta, rho = coef[0:1], coef[1:2], coef[2:3]
            rho_new = 1.0 / (2.0 * sigma - rho)
            keep = (rho_new * rho).reshape(1, 1, nb)
            gain = (2.0 * rho_new / delta).reshape(1, 1, nb)
            step = keep * step_ref[...] + gain * inv[...] * resid
            step_ref[...] = step
            field[0:ex, 0:ey] = field[0:ex, 0:ey] + step
            coef[2:3] = rho_new

        return 0

    lax.fori_loop(0, PASSES, one_pass, 0)
    x_out[...] = field[0:ex, 0:ey]
    ahead[...] = rhs[...] - ahead[...]

    def project(i, _):
        for j in range(ey):
            e = i * ey + j
            dots = jnp.sum(wall[e] * ahead[i, pl.ds(j, 1), :], axis=1, keepdims=True)
            proj[e] = jnp.where(lane == sub, dots, 0.0)
        return 0

    lax.fori_loop(0, ex, project, 0)
    at_t = hot_at[...].reshape(ne * 8, 128).T[:AGG_DEV]
    crhs_own[...] = mul_left_hot(at_t, proj[...].reshape(ne * 8, 128))
    crhs_copy = remote(crhs_own, gath2.at[q], crhs_send, crhs_recv.at[q], gy=0 * q)

    @pl.when(q > 0)
    def _():
        crhs_copy.start()
        rows_out[...] = jnp.zeros_like(rows_out)
        crhs_out[...] = jnp.zeros_like(crhs_out)
        rows_copy.wait_send()
        crhs_copy.wait_send()

    @pl.when(q == 0)
    def _():
        gath[0] = rows_own[...]
        gath2[0] = crhs_own[...]
        for n in range(1, gys):
            remote(rows_own, gath.at[n], rows_send, rows_recv.at[n], gy=0 * q).wait_recv()
        p_shape = (cap * 8, AGG_DEV * 8)
        p_row = iota(p_shape, 0)
        p_col = iota(p_shape, 1)
        shift = (lax.shift_right_logical(p_row, 3) - lax.shift_right_logical(p_col, 3)).astype(F32)
        a_index = lax.shift_right_logical(p_col, 3).astype(F32)
        same_m = (p_row & 7) == (p_col & 7)
        s_shape = (cap, AGG_DEV)
        s_shift = (iota(s_shape, 0) - iota(s_shape, 1)).astype(F32)
        s_index = iota(s_shape, 1).astype(F32)
        offset = jnp.zeros((1, 1), F32)
        packed = jnp.zeros((cap * 8, 384), F32)
        places = []
        for n in range(gys):
            number = gath[n, 0:1, 288:289]
            hot = jnp.where((shift == offset) & same_m & (a_index < number), 1.0, 0.0)
            packed = packed + mul_left_hot(hot, gath[n])
            places.append(jnp.where((s_shift == offset) & (s_index < number), 1.0, 0.0))
            offset = offset + number
        rows_out[...] = packed.reshape(cap, 8, 384)[:, :MODES, :288]
        for n in range(1, gys):
            remote(crhs_own, gath2.at[n], crhs_send, crhs_recv.at[n], gy=0 * q).wait_recv()
        packed_rhs = jnp.zeros((cap, 128), F32)
        for n in range(gys):
            packed_rhs = packed_rhs + mul_left_hot(places[n], gath2[n])
        crhs_out[...] = packed_rhs[:, :MODES]


def solution(mesh):
    gxs, gys = mesh.shape["gx"], mesh.shape["gy"]

    def per_device(rhs, diag_blocks, east_blocks, north_blocks, face_open, modes, aggregate, live_count):
        ex, ey, nb = rhs.shape
        ne = ex * ey
        cap = gys * AGG_DEV
        block = (ex, ey, nb, nb)
        dma = pltpu.SemaphoreType.DMA

        def vmem(*shape):
            return pltpu.VMEM(shape, F32)

        x, rows, crhs = pl.pallas_call(
            functools.partial(kernel, (gxs, gys, ex, ey, nb)),
            out_shape=(
                jax.ShapeDtypeStruct((ex, ey, nb), F32),
                jax.ShapeDtypeStruct((cap, MODES, 288), F32),
                jax.ShapeDtypeStruct((cap, MODES), F32),
            ),
            in_specs=[
                pl.BlockSpec(memory_space=pltpu.VMEM),
                pl.BlockSpec(memory_space=pl.ANY),
                pl.BlockSpec(memory_space=pl.ANY),
                pl.BlockSpec(memory_space=pl.ANY),
                pl.BlockSpec(memory_space=pltpu.SMEM),
                pl.BlockSpec(memory_space=pltpu.VMEM),
                pl.BlockSpec(memory_space=pltpu.SMEM),
                pl.BlockSpec(memory_space=pltpu.SMEM),
            ],
            out_specs=[pl.BlockSpec(memory_space=pltpu.VMEM)] * 3,
            scratch_shapes=[
                vmem(*block), vmem(*block), vmem(*block),
                vmem(ex, ey, nb), vmem(ex + 1, ey + 8, nb), vmem(ex, ey, nb),
                vmem(ex + 1, ey, nb), vmem(ex, ey + 8, nb), vmem(ex, ey, nb), vmem(8, nb),
                vmem(ne + 16, 8, nb), vmem(ne + 16, 8, 128), vmem(ne, 8, 128), vmem(ne, 8, 128),
                vmem(ne + 16, 8, 384), vmem(ne, 8, nb), vmem(ne, 8, nb), vmem(ne, 8, nb),
                vmem(ex, 8, nb), vmem(ex, 8, 128), vmem(8, nb), vmem(8, nb),
                vmem(PASSES, ey, nb), vmem(PASSES, 8, nb), vmem(PASSES, ey, nb), vmem(PASSES, 8, nb),
                vmem(2, ey, 128), vmem(2, ey, 128), vmem(gys - 1, 2, ey, 128), vmem(gxs - 1, 2, ey, 128),
                vmem(gys, 128, 384), vmem(gys, AGG_DEV, 128), vmem(128, 384), vmem(AGG_DEV, 128),
                vmem(ne, 8, 128),
                dma((ex, 3)), dma((PASSES, 4)), dma((PASSES, 4)), dma((4,)), dma((4,)),
                dma((gys - 1,)), dma((gys - 1,)), dma((gxs - 1,)), dma((gxs - 1,)),
                dma, dma((gys,)), dma, dma((gys,)),
            ],
            compiler_params=pltpu.CompilerParams(
                collective_id=0, has_side_effects=True, vmem_limit_bytes=60 << 20
            ),
        )(rhs, diag_blocks, east_blocks, north_blocks, face_open, modes, aggregate, live_count)
        return x, rows[None, None], crhs[None, None]

    in_specs = (
        P("gx", "gy", None),
        P("gx", "gy", None, None),
        P("gx", "gy", None, None),
        P("gx", "gy", None, None),
        P("gx", "gy", None),
        P("gx", "gy", None, None),
        P("gx", "gy"),
        P("gx", "gy"),
    )
    out_specs = (P("gx", "gy", None), P("gx", "gy", None, None, None), P("gx", "gy", None, None))
    return jax.shard_map(
        per_device, mesh=mesh, in_specs=in_specs, out_specs=out_specs, check_vma=False
    )
```

profile of v0, /device:TPU:0, one launch (start us, length us, event | category | flops | bytes accessed | tf_op | source)
XLA Modules:
  0.0 58.8 jit_solution(911032471315548459)
XLA Ops:
  1.3 1.4 %copy.11.face = s32[6,8,2]{2,1,0:T(8,128)} copy(s32[6,8,2]{1,2,0:T(2,128)} %param.12) | data formatting | bytes 768 | tf_op args[4]
  2.7 1.8 %copy.12.modes = f32[6,8,6,192]{3,2,1,0:T(8,128)} copy(f32[6,8,6,192]{3,1,2,0:T(8,128)} %param.13) | data formatting | bytes 442368 | tf_op args[5]
  4.5 49.4 %shard_map.103 = (f32[6,8,192]{2,1,0:T(8,128)}, f32[64,6,288]{2,1,0:T(8,128)}, f32[64,6]{1,0:T(8,128)}) custom-call(f32[6,8,192]{2,1,0:T(8,128)} %rhs.1, f32[6,8,192,192]{3,2,1,0:T(8,128)} %diag_hbm.1, f32[6,8,192,192]{3,2,1,0:T(8,128)} %east_hbm.1, f32[6,8,192,192]{3,2,1,0:T(8,128)} %north_hbm.1, s32[6,8,2]{2,1,0:T(8,128)} %copy.11.face, ...), custom_call_target="tpu_custom_call" | custom-call | tf_op jit(solution)/shard_map/pallas_call | solution.py:413
  53.9 2.1 %copy.13 = f32[1,1,64,6,288]{4,2,3,1,0:T(8,128)} copy(f32[1,1,64,6,288]{4,3,2,1,0:T(8,128)} %bitcast.2) | data formatting | bytes 884736
  56.0 1.4 %copy.14 = f32[1,1,64,6]{2,1,3,0:T(1,128)} copy(f32[1,1,64,6]{3,2,1,0:T(8,128)} %bitcast.3) | data formatting | bytes 3072
  57.4 1.4 %copy.17 = f32[6,8,192]{2,1,0:T(8,128)} copy(f32[6,8,192]{2,1,0:T(8,128)} %get-tuple-element.15) | data formatting | bytes 73728
where the time goes:
time: 59.2 us; the launch traced here: 58.8 us
  Pallas kernels  49.4 us (83%)
  local copies, waits for them, and re-layouts  8.1 us (14%)
  between operations  1.29 us (2%)
    pallas_call x1, Pallas kernels, per_device(): pl.pallas_call(functools.partial(kernel, (gxs, gys, ex, ey, nb)), out_sha...  49.4 us
    unnamed x5, local copies, waits for them, and re-layouts  8.1 us

commit v1 on v0

--- a/solution.py
+++ b/solution.py
@@ -11,6 +11,7 @@
 CHEB = 4
 AGG_DEV = 16
 PASSES = CHEB + 1
+CHUNK = 48
 F32 = jnp.float32
 BF16 = jnp.bfloat16
 NN = (((1,), (0,)), ((), ()))
@@ -51,19 +52,18 @@
 def kernel(
     sizes,
     rhs, diag_hbm, east_hbm, north_hbm, face, modes, aggregate, live,
-    x_out, rows_out, crhs_out,
-    diag, east, north, inv, field, ahead, back_x, back_y, step_ref, coef,
+    x_out, gath, gath2,
+    diag, east, north, pack, inv, field, main_ref, ahead, back_x, back_y, step_ref, coef,
     wall, hot6, hot8, hot_at, wide_hot, r_diag, r_east, r_north,
     w_stage, q_stage, v_stage, y_stage,
     v_east, v_north, b_west, b_south,
-    sum_own, sum_own2, sum_gy, sum_gx, gath, gath2, rows_own, crhs_own, proj,
+    sum_own, sum_own2, sum_gy, sum_gx, rows_own, crhs_own, proj,
     load_sem, halo_send, halo_recv, mode_send, mode_recv,
     gy_send, gy_recv, gx_send, gx_recv, rows_send, rows_recv, crhs_send, crhs_recv,
 ):
     gxs, gys, ex, ey, nb = sizes
     ne = ex * ey
     slots = ne + 16
-    cap = gys * AGG_DEV
     g = lax.axis_index("gx")
     q = lax.axis_index("gy")
 
@@ -97,9 +97,11 @@
         for j in range(ey):
             e = i * ey + j
             slot = aggregate[i, j]
-            wall[e] = jnp.concatenate([modes[i, j], jnp.zeros((8 - MODES, nb), F32)], 0)
+            wall[e, MODES:] = jnp.zeros((8 - MODES, nb), F32)
+            for m in range(MODES):
+                wall[e, m : m + 1, :] = modes[i, m, j : j + 1, :]
             hot6[e] = jnp.where((lane == MODES * slot + sub) & (sub < MODES), 1.0, 0.0)
-            hot8[e] = jnp.where(lane == 8 * slot + sub, 1.0, 0.0)
+            hot8[e] = jnp.where(lane == AGG_DEV * sub + slot, 1.0, 0.0)
             hot_at[e] = jnp.where(lane == slot, 1.0, 0.0)
             wide_hot[e] = jnp.where((lane3 == MODES * slot + sub3) & (sub3 < MODES), 1.0, 0.0)
         w_stage[i] = wall[i * ey]
@@ -131,6 +133,102 @@
     )
     for sends, _, copy in mode_copies:
         pl.when(sends)(copy.start)
+
+    half = nb // 2
+
+    def fold(value):
+        return jnp.sum(value.reshape(-1, 8, 128), axis=0)
+
+    def down(value):
+        return jnp.sum(value, axis=0, keepdims=True)
+
+    def element(i, j, local, forward):
+        at = pl.ds(j, 1)
+        ox = face[i, 0, j].astype(F32)
+        oy = face[i, 1, j].astype(F32)
+        if local:
+            column = jnp.broadcast_to(field[i, at, :], (128, nb)).T
+        if forward:
+            ve = field[i + 1, at, :] * ox
+            vn = field[i, pl.ds(j + 1, 1), :] * oy
+            vb = jnp.concatenate([ve[:, 128:], vn[:, 128:]], 1)
+            ve, vn = ve[:, :128], vn[:, :128]
+        parts = []
+        sums = [jnp.zeros((8, 128), F32)] * 5
+        for c in range(0, nb, CHUNK):
+            ea = east[i, j, c : c + CHUNK, 0:128]
+            na = north[i, j, c : c + CHUNK, 0:128]
+            pa = pack[i, j, c : c + CHUNK, :]
+            if local:
+                col = column[c : c + CHUNK]
+                sums[0] = sums[0] + fold(ea * col)
+                sums[1] = sums[1] + fold(na * col)
+                sums[2] = sums[2] + fold(pa * col)
+                sums[3] = sums[3] + fold(diag[i, j, c : c + CHUNK, 0:128] * col)
+                if c < half:
+                    other = column[c + half : c + half + CHUNK]
+                    mixed = jnp.where(iota(col.shape, 1) < nb - 128, col, other)
+                    sums[4] = sums[4] + fold(pack[i, j, nb + c : nb + c + CHUNK, :] * mixed)
+            if forward:
+                parts.append(ea * ve + na * vn + pa * vb)
+        if local:
+            shared = down(sums[2])
+            back_x[i + 1, at, 0:128] = ox * down(sums[0])
+            back_x[i + 1, at, 128:nb] = ox * shared[:, :64]
+            back_y[i, pl.ds(j + 1, 1), 0:128] = oy * down(sums[1])
+            back_y[i, pl.ds(j + 1, 1), 128:nb] = oy * shared[:, 64:]
+            tail = down(sums[4])
+            main_ref[i, at, 0:128] = down(sums[3])
+            main_ref[i, at, 128:nb] = tail[:, :64] + tail[:, 64:]
+        if forward:
+            ahead[i, at, :] = down(jnp.concatenate(parts, 0).T)
+
+    last_x, last_y = ex - 1, ey - 1
+
+    def halo_copies(k):
+        return (
+            remote(field.at[0, pl.ds(0, ey)], v_east.at[k], halo_send.at[k, 0], halo_recv.at[k, 0], gx=west),
+            remote(v_stage, v_north.at[k], halo_send.at[k, 1], halo_recv.at[k, 1], gy=south),
+            remote(back_x.at[ex], b_west.at[k], halo_send.at[k, 2], halo_recv.at[k, 2], gx=east_g),
+            remote(y_stage, b_south.at[k], halo_send.at[k, 3], halo_recv.at[k, 3], gy=north_q),
+        )
+
+    def send_rims(go_w, go_s):
+        for i in range(ex):
+            v_stage[pl.ds(i, 1), :] = field[i, 0:1, :]
+        pl.when(has_west)(go_w.start)
+        pl.when(has_south)(go_s.start)
+
+    def take_rims(k, go_w, go_s):
+        pl.when(has_east)(go_w.wait_recv)
+        pl.when(has_north)(go_s.wait_recv)
+        field[ex, 0:ey] = v_east[k]
+        for i in range(ex):
+            field[i, ey : ey + 1, :] = v_north[k, i : i + 1, :]
+
+    def send_north(go_n):
+        for i in range(ex):
+            y_stage[pl.ds(i, 1), :] = back_y[i, ey : ey + 1, :]
+        pl.when(has_north)(go_n.start)
+
+    def finish(k, copies):
+        go_w, go_s, go_e, go_n = copies
+        pl.when(has_west)(go_e.wait_recv)
+        pl.when(has_south)(go_n.wait_recv)
+        back_x[0] = b_west[k]
+        for i in range(ex):
+            back_y[i, 0:1, :] = b_south[k, i : i + 1, :]
+        pl.when(has_west)(go_w.wait_send)
+        pl.when(has_south)(go_s.wait_send)
+        pl.when(has_east)(go_e.wait_send)
+        pl.when(has_north)(go_n.wait_send)
+        applied = main_ref[...] + ahead[...] + back_x[0:ex] + back_y[:, 0:ey]
+        ahead[...] = applied
+        return applied
+
+    first = halo_copies(0)
+    send_rims(first[0], first[1])
+    take_rims(0, first[0], first[1])
 
     same = iota((nb, nb), 0) == iota((nb, nb), 1)
 
@@ -146,16 +244,21 @@
             both = jnp.concatenate([w_high, w - w_high], 0).astype(BF16)
             for block, result, scale in (
                 (diag, r_diag, None),
-                (east, r_east, face[i, j, 0].astype(F32)),
-                (north, r_north, face[i, j, 1].astype(F32)),
+                (east, r_east, face[i, 0, j].astype(F32)),
+                (north, r_north, face[i, 1, j].astype(F32)),
             ):
                 high, low = split(block[i, j])
                 product = mul(both, high, NN) + mul(both, low, NN)
                 product = product[:8] + product[8:]
                 result[e] = product if scale is None else product * scale
+            pack[i, j, 0:nb, :] = jnp.concatenate([east[i, j, :, 128:nb], north[i, j, :, 128:nb]], 1)
+            pack[i, j, nb:, :] = jnp.concatenate([diag[i, j, 0:half, 128:nb], diag[i, j, half:nb, 128:nb]], 1)
+            element(i, j, True, True)
         return 0
 
     lax.fori_loop(0, ex, coarse_row, 0)
+    pl.when(has_east)(first[2].start)
+    send_north(first[3])
 
     for sends, receives, copy in mode_copies:
         pl.when(receives)(copy.wait_recv)
@@ -197,62 +300,34 @@
         for k in range(1, gxs)
     ]
 
-    def backs(i, j):
-        own = field[i, pl.ds(j, 1), :]
-        column = jnp.broadcast_to(own, (128, nb)).T
-        short = column[:, : nb - 128]
-        ox = face[i, j, 0].astype(F32)
-        oy = face[i, j, 1].astype(F32)
-        for block, result, at, scale in (
-            (east, back_x, (i + 1, pl.ds(j, 1)), ox),
-            (north, back_y, (i, pl.ds(j + 1, 1)), oy),
-        ):
-            result[at + (slice(0, 128),)] = scale * jnp.sum(block[i, j, :, 0:128] * column, axis=0, keepdims=True)
-            result[at + (slice(128, nb),)] = scale * jnp.sum(block[i, j, :, 128:nb] * short, axis=0, keepdims=True)
-
-    def aheads(i, j):
-        ox = face[i, j, 0].astype(F32)
-        oy = face[i, j, 1].astype(F32)
-        own = field[i, pl.ds(j, 1), :]
-        ve = field[i + 1, pl.ds(j, 1), :] * ox
-        vn = field[i, pl.ds(j + 1, 1), :] * oy
-
-        def part(s, t):
-            cut = slice(s, t)
-            return (
-                diag[i, j, :, cut] * own[:, cut]
-                + east[i, j, :, cut] * ve[:, cut]
-                + north[i, j, :, cut] * vn[:, cut]
-            )
-
-        rest = jnp.concatenate([part(128, nb), jnp.zeros((nb, 256 - nb), F32)], 1)
-        total = part(0, 128) + rest
-        ahead[i, pl.ds(j, 1), :] = jnp.sum(total.T, axis=0, keepdims=True)
-
-    last_x, last_y = ex - 1, ey - 1
+    applied = finish(0, first)
+    scaled = inv[...] * applied
+    base = rhs[...]
+
+    def squares(value):
+        value = jnp.sum(value * value, axis=0)
+        rest = jnp.concatenate([value[:, 128:], jnp.zeros((ey, 256 - nb), F32)], 1)
+        return value[:, :128] + rest
+
+    sum_own[0] = squares(scaled)
+    sum_own[1] = squares(base)
+    for copy in sum_copies_gy:
+        copy.start()
+    field[0:ex, 0:ey] = inv[...] * base
 
     def one_pass(k, _):
-        for i in range(ex):
-            v_stage[pl.ds(i, 1), :] = field[i, 0:1, :]
-        go_w = remote(field.at[0, pl.ds(0, ey)], v_east.at[k], halo_send.at[k, 0], halo_recv.at[k, 0], gx=west)
-        go_s = remote(v_stage, v_north.at[k], halo_send.at[k, 1], halo_recv.at[k, 1], gy=south)
-        go_e = remote(back_x.at[ex], b_west.at[k], halo_send.at[k, 2], halo_recv.at[k, 2], gx=east_g)
-        go_n = remote(y_stage, b_south.at[k], halo_send.at[k, 3], halo_recv.at[k, 3], gy=north_q)
-        pl.when(has_west)(go_w.start)
-        pl.when(has_south)(go_s.start)
+        copies = halo_copies(k)
+        send_rims(copies[0], copies[1])
         for j in range(ey):
-            backs(last_x, j)
-        pl.when(has_east)(go_e.start)
+            element(last_x, j, True, False)
+        pl.when(has_east)(copies[2].start)
         for i in range(last_x):
-            backs(i, last_y)
-        for i in range(ex):
-            y_stage[pl.ds(i, 1), :] = back_y[i, ey : ey + 1, :]
-        pl.when(has_north)(go_n.start)
+            element(i, last_y, True, False)
+        send_north(copies[3])
 
         def inner(i, _):
             for j in range(last_y):
-                backs(i, j)
-                aheads(i, j)
+                element(i, j, True, True)
             return 0
 
         lax.fori_loop(0, last_x, inner, 0)
@@ -267,42 +342,12 @@
             for copy in sum_copies_gx:
                 copy.start()
 
-        pl.when(has_east)(go_w.wait_recv)
-        pl.when(has_north)(go_s.wait_recv)
-        field[ex, 0:ey] = v_east[k]
-        for i in range(ex):
-            field[i, ey : ey + 1, :] = v_north[k, i : i + 1, :]
+        take_rims(k, copies[0], copies[1])
         for j in range(ey):
-            aheads(last_x, j)
+            element(last_x, j, False, True)
         for i in range(last_x):
-            aheads(i, last_y)
-        pl.when(has_west)(go_e.wait_recv)
-        pl.when(has_south)(go_n.wait_recv)
-        back_x[0] = b_west[k]
-        for i in range(ex):
-            back_y[i, 0:1, :] = b_south[k, i : i + 1, :]
-        pl.when(has_west)(go_w.wait_send)
-        pl.when(has_south)(go_s.wait_send)
-        pl.when(has_east)(go_e.wait_send)
-        pl.when(has_north)(go_n.wait_send)
-        applied = ahead[...] + back_x[0:ex] + back_y[:, 0:ey]
-        ahead[...] = applied
-
-        @pl.when(k == 0)
-        def _():
-            scaled = inv[...] * applied
-            base = rhs[...]
-
-            def fold(value):
-                value = jnp.sum(value * value, axis=0)
-                rest = jnp.concatenate([value[:, 128:], jnp.zeros((ey, 256 - nb), F32)], 1)
-                return value[:, :128] + rest
-
-            sum_own[0] = fold(scaled)
-            sum_own[1] = fold(base)
-            for copy in sum_copies_gy:
-                copy.start()
-            field[0:ex, 0:ey] = inv[...] * base
+            element(i, last_y, False, True)
+        finish(k, copies)
 
         @pl.when(k == 1)
         def _():
@@ -340,7 +385,7 @@
 
         return 0
 
-    lax.fori_loop(0, PASSES, one_pass, 0)
+    lax.fori_loop(1, PASSES, one_pass, 0)
     x_out[...] = field[0:ex, 0:ey]
     ahead[...] = rhs[...] - ahead[...]
 
@@ -359,8 +404,6 @@
     @pl.when(q > 0)
     def _():
         crhs_copy.start()
-        rows_out[...] = jnp.zeros_like(rows_out)
-        crhs_out[...] = jnp.zeros_like(crhs_out)
         rows_copy.wait_send()
         crhs_copy.wait_send()
 
@@ -370,31 +413,38 @@
         gath2[0] = crhs_own[...]
         for n in range(1, gys):
             remote(rows_own, gath.at[n], rows_send, rows_recv.at[n], gy=0 * q).wait_recv()
-        p_shape = (cap * 8, AGG_DEV * 8)
-        p_row = iota(p_shape, 0)
-        p_col = iota(p_shape, 1)
-        shift = (lax.shift_right_logical(p_row, 3) - lax.shift_right_logical(p_col, 3)).astype(F32)
-        a_index = lax.shift_right_logical(p_col, 3).astype(F32)
-        same_m = (p_row & 7) == (p_col & 7)
-        s_shape = (cap, AGG_DEV)
-        s_shift = (iota(s_shape, 0) - iota(s_shape, 1)).astype(F32)
-        s_index = iota(s_shape, 1).astype(F32)
+            remote(crhs_own, gath2.at[n], crhs_send, crhs_recv.at[n], gy=0 * q).wait_recv()
+
+
+def packing(gys, x_in, gath, gath2, x_out, rows_out, crhs_out):
+    cap = gys * AGG_DEV
+    q = lax.axis_index("gy")
+    x_out[...] = x_in[...]
+
+    @pl.when(q > 0)
+    def _():
+        rows_out[...] = jnp.zeros_like(rows_out)
+        crhs_out[...] = jnp.zeros_like(crhs_out)
+
+    @pl.when(q == 0)
+    def _():
+        slot = iota((cap, cap), 0).astype(F32)
+        source = iota((cap, cap), 1)
+        owner = lax.shift_right_logical(source, AGG_DEV.bit_length() - 1)
+        index = (source & (AGG_DEV - 1)).astype(F32)
         offset = jnp.zeros((1, 1), F32)
-        packed = jnp.zeros((cap * 8, 384), F32)
-        places = []
+        hot = jnp.zeros((cap, cap), F32)
         for n in range(gys):
             number = gath[n, 0:1, 288:289]
-            hot = jnp.where((shift == offset) & same_m & (a_index < number), 1.0, 0.0)
-            packed = packed + mul_left_hot(hot, gath[n])
-            places.append(jnp.where((s_shift == offset) & (s_index < number), 1.0, 0.0))
+            hit = (owner == n) & (slot == index + offset) & (index < number)
+            hot = jnp.where(hit, 1.0, hot)
             offset = offset + number
-        rows_out[...] = packed.reshape(cap, 8, 384)[:, :MODES, :288]
-        for n in range(1, gys):
-            remote(crhs_own, gath2.at[n], crhs_send, crhs_recv.at[n], gy=0 * q).wait_recv()
-        packed_rhs = jnp.zeros((cap, 128), F32)
-        for n in range(gys):
-            packed_rhs = packed_rhs + mul_left_hot(places[n], gath2[n])
-        crhs_out[...] = packed_rhs[:, :MODES]
+        for m in range(MODES):
+            stacked = jnp.concatenate([gath[n, m * AGG_DEV : (m + 1) * AGG_DEV, :] for n in range(gys)], 0)
+            rows_out[m] = mul_left_hot(hot, stacked)[:, :288]
+        packed = mul_left_hot(hot, gath2[...].reshape(cap, 128)).T
+        for m in range(MODES):
+            crhs_out[m] = packed[m : m + 1]
 
 
 def solution(mesh):
@@ -410,12 +460,12 @@
         def vmem(*shape):
             return pltpu.VMEM(shape, F32)
 
-        x, rows, crhs = pl.pallas_call(
+        x, gathered, gathered_rhs = pl.pallas_call(
             functools.partial(kernel, (gxs, gys, ex, ey, nb)),
             out_shape=(
                 jax.ShapeDtypeStruct((ex, ey, nb), F32),
-                jax.ShapeDtypeStruct((cap, MODES, 288), F32),
-                jax.ShapeDtypeStruct((cap, MODES), F32),
+                jax.ShapeDtypeStruct((gys, 128, 384), F32),
+                jax.ShapeDtypeStruct((gys, AGG_DEV, 128), F32),
             ),
             in_specs=[
                 pl.BlockSpec(memory_space=pltpu.VMEM),
@@ -429,15 +479,15 @@
             ],
             out_specs=[pl.BlockSpec(memory_space=pltpu.VMEM)] * 3,
             scratch_shapes=[
-                vmem(*block), vmem(*block), vmem(*block),
-                vmem(ex, ey, nb), vmem(ex + 1, ey + 8, nb), vmem(ex, ey, nb),
+                vmem(*block), vmem(*block), vmem(*block), vmem(ex, ey, nb + nb // 2, 128),
+                vmem(ex, ey, nb), vmem(ex + 1, ey + 8, nb), vmem(ex, ey, nb), vmem(ex, ey, nb),
                 vmem(ex + 1, ey, nb), vmem(ex, ey + 8, nb), vmem(ex, ey, nb), vmem(8, nb),
                 vmem(ne + 16, 8, nb), vmem(ne + 16, 8, 128), vmem(ne, 8, 128), vmem(ne, 8, 128),
                 vmem(ne + 16, 8, 384), vmem(ne, 8, nb), vmem(ne, 8, nb), vmem(ne, 8, nb),
                 vmem(ex, 8, nb), vmem(ex, 8, 128), vmem(8, nb), vmem(8, nb),
                 vmem(PASSES, ey, nb), vmem(PASSES, 8, nb), vmem(PASSES, ey, nb), vmem(PASSES, 8, nb),
                 vmem(2, ey, 128), vmem(2, ey, 128), vmem(gys - 1, 2, ey, 128), vmem(gxs - 1, 2, ey, 128),
-                vmem(gys, 128, 384), vmem(gys, AGG_DEV, 128), vmem(128, 384), vmem(AGG_DEV, 128),
+                vmem(128, 384), vmem(AGG_DEV, 128),
                 vmem(ne, 8, 128),
                 dma((ex, 3)), dma((PASSES, 4)), dma((PASSES, 4)), dma((4,)), dma((4,)),
                 dma((gys - 1,)), dma((gys - 1,)), dma((gxs - 1,)), dma((gxs - 1,)),
@@ -446,8 +496,22 @@
             compiler_params=pltpu.CompilerParams(
                 collective_id=0, has_side_effects=True, vmem_limit_bytes=60 << 20
             ),
-        )(rhs, diag_blocks, east_blocks, north_blocks, face_open, modes, aggregate, live_count)
-        return x, rows[None, None], crhs[None, None]
+        )(
+            rhs, diag_blocks, east_blocks, north_blocks,
+            jnp.transpose(face_open, (0, 2, 1)), jnp.transpose(modes, (0, 2, 1, 3)), aggregate, live_count,
+        )
+        x, rows, crhs = pl.pallas_call(
+            functools.partial(packing, gys),
+            out_shape=(
+                jax.ShapeDtypeStruct((ex, ey, nb), F32),
+                jax.ShapeDtypeStruct((MODES, cap, 288), F32),
+                jax.ShapeDtypeStruct((MODES, 1, cap), F32),
+            ),
+            in_specs=[pl.BlockSpec(memory_space=pltpu.VMEM)] * 3,
+            out_specs=[pl.BlockSpec(memory_space=pltpu.VMEM)] * 3,
+        )(x, gathered, gathered_rhs)
+        rows = jnp.transpose(rows, (1, 0, 2))
+        return x, rows[None, None], jnp.transpose(crhs[None], (0, 2, 3, 1))
 
     in_specs = (
         P("gx", "gy", None),

time: 59.2 us -> 57 us (0.963)
  local copies, waits for them, and re-layouts: 8.1 us -> 0 us
  Pallas kernels: 49.4 us -> 55.6 us
    unnamed x5 -> x0, local copies, waits for them, and re-layouts: 8.1 us -> none
    pallas_call x1, Pallas kernels: 49.4 us -> 53.2 us  [per_device(): pl.pallas_call(functools.partial(kernel, (gxs, gys, ex, ey, nb)), out_sha...]
    pallas_call x0 -> x1, Pallas kernels: none -> 2.4 us  [per_device(): pl.pallas_call(functools.partial(packing, gys), out_shape=(jax.ShapeDtype...]
where the time goes in v1:
time: 57 us; the launch traced here: 56.9 us
  Pallas kernels  55.6 us (98%)
  between operations  1.29 us (2%)
    pallas_call x1, Pallas kernels, per_device(): pl.pallas_call(functools.partial(kernel, (gxs, gys, ex, ey, nb)), out_sha...  53.2 us
    pallas_call x1, Pallas kernels, per_device(): pl.pallas_call(functools.partial(packing, gys), out_shape=(jax.ShapeDtype...  2.4 us

profile of v1, /device:TPU:0, one launch (start us, length us, event | category | flops | bytes accessed | tf_op | source)
XLA Modules:
  0.0 56.9 jit_solution(2434112304808335566)
XLA Ops:
  1.3 53.2 %shard_map.103 = (f32[6,8,192]{2,1,0:T(8,128)}, f32[4,128,384]{2,1,0:T(8,128)}, f32[4,16,128]{2,1,0:T(8,128)}) custom-call(f32[6,8,192]{2,1,0:T(8,128)} %rhs.1, f32[6,8,192,192]{3,2,1,0:T(8,128)} %diag_hbm.1, f32[6,8,192,192]{3,2,1,0:T(8,128)} %east_hbm.1, f32[6,8,192,192]{3,2,1,0:T(8,128)} %north_hbm.1, s32[6,2,8]{2,1,0:T(2,128)} %bitcast.9, ...), custom_call_target="tpu_custom_call" | custom-call | tf_op jit(solution)/shard_map/pallas_call | solution.py:463
  54.5 2.4 %shard_map.104 = (f32[6,8,192]{2,1,0:T(8,128)}, f32[6,64,288]{2,1,0:T(8,128)}, f32[6,1,64]{2,1,0:T(1,128)}) custom-call(f32[6,8,192]{2,1,0:T(8,128)} %get-tuple-element.9.x_in, f32[4,128,384]{2,1,0:T(8,128)} %get-tuple-element.10.gath, f32[4,16,128]{2,1,0:T(8,128)} %get-tuple-element.11.gath2), custom_call_target="tpu_custom_call" | custom-call | tf_op jit(solution)/shard_map/pallas_call | solution.py:503
